TPU v7x, 128 devices: a whole 4x4x4 slice. The times are simulated.
128 devices in a mesh: gx: 16 (over z_lo, y, core), gy: 8 (over x, z_hi).
Axes of the slice: x: 4, y: 4, z: 4 (z_hi: 2, z_lo: 2; z = z_hi * 2 + z_lo), core: 2. Of those that a mesh axis runs over, the one named last changes fastest.
Arguments:
- queries: bfloat16 [64, 512, 1024], P('gy', 'gx'), may hold values from -8 to 8
- keys: bfloat16 [64, 512, 1024], P('gy', 'gx'), may hold values from -8 to 8
- values: bfloat16 [64, 512, 1024], P('gy', 'gx'), may hold values from -6 to 6
- out_grad: bfloat16 [64, 512, 1024], P('gy', 'gx'), may hold values from -6 to 6
- tissue: int32 [64, 512], P('gy', 'gx'), may hold values from 0 to 1, as said below
Outputs:
- attended: bfloat16 [64, 512, 1024], P('gy', 'gx')
- query_grad: bfloat16 [64, 512, 1024], P('gy', 'gx')
- key_grad: bfloat16 [64, 512, 1024], P('gy', 'gx')
- value_grad: bfloat16 [64, 512, 1024], P('gy', 'gx')
Inputs may be any that keep to these rules, and one draw needn't show every extreme that they name: `tissue`: in each device's tile of 8 x 32 tokens the live tokens lie within one band of whole rows of the tile; the tile at the grid's first 8 rows and first 32 columns is all live.
All inputs are finite; a program needn't handle non-finite values.
Results may differ from a plain program's by a relative error of at most 0.039.
Values may be sent and summed in bfloat16 or wider, within the bound.
A program may use at most 128 MiB of HBM per device.

v0:
```python
import functools

import jax
import jax.numpy as jnp
from jax import lax
from jax.experimental import pallas as pl
from jax.experimental.pallas import tpu as pltpu
from jax.sharding import PartitionSpec as P

MESH = pl.DeviceIdType.MESH
HD = 64
RAD = 6
TH = 8
TW = 32
LANES = 128
OWN = TH * TW
STRIP = RAD * TW
CENTER = OWN + 2 * STRIP
SPAN = TH + 2 * RAD
SLOTS = 128
KEYS = CENTER + 2 * SLOTS
FAR = -1e30
BF = jnp.bfloat16
F32 = jnp.float32


def iota(shape, dim):
    return lax.broadcasted_iota(jnp.int32, shape, dim)


def slot_row(slot):
    return jnp.floor((slot.astype(F32) + 0.5) * (1.0 / RAD)).astype(jnp.int32)


def select_rows(shape, slot_dim):
    slot_all, token = iota(shape, slot_dim), iota(shape, 1 - slot_dim)
    right = slot_all >= SLOTS
    slot = jnp.where(right, slot_all - SLOTS, slot_all)
    row = slot_row(slot)
    col = slot - row * RAD + jnp.where(right, TW - RAD, 0)
    hit = (slot < SPAN * RAD) & (token == row * TW + col)
    return jnp.where(hit, 1.0, 0.0).astype(BF)


def key_features(row, col, tile_col, padded, dead_tile):
    count = row.shape[0]
    lane = iota((count, LANES), 1)
    tile_row = jnp.where(
        row < RAD, 16 + TH - RAD + row, jnp.where(row < RAD + TH, row - RAD, 32 + row - RAD - TH)
    )
    pick = jnp.where(lane == tile_row, 1.0, 0.0).astype(BF)
    dead = jnp.dot(pick, dead_tile, preferred_element_type=F32)
    dead_part = jnp.where(lane == tile_col, dead, 0.0)
    row_part = jnp.where(jnp.abs(row - RAD - (lane - 32)) > RAD, 1.0, 0.0)
    col_part = jnp.where(jnp.abs(col - (lane - 40)) > RAD, 1.0, 0.0)
    pad_part = jnp.where((lane == 72) & padded, 1.0, 0.0)
    out = jnp.where(
        lane < 32, dead_part, jnp.where(lane < 40, row_part, jnp.where(lane < 72, col_part, pad_part))
    )
    return (out * FAR).astype(BF)


def kernel(
    groups, nx, ny,
    k_hbm, v_hbm, q_hbm, g_hbm, tissue_ref,
    o_hbm, dq_hbm, dk_hbm, dv_hbm,
    kv, q_buf, g_buf, feat, qfeat, sel, sel_t, dead, dead32, live_q,
    hsend, centre, own, hret_out, hret_in, vret_out, vret_in,
    o_buf, dq_buf, dk_buf, dv_buf,
    in_sem, out_sem, vf_send, vf_recv, hf_send, hf_recv, hr_send, hr_recv, vr_send, vr_recv,
    lv_send, lv_recv, lh_send, lh_recv,
):
    gx, gy = lax.axis_index("gx"), lax.axis_index("gy")
    has_up, has_down = gy > 0, gy < ny - 1
    has_left, has_right = gx > 0, gx < nx - 1
    up = (gx, jnp.maximum(gy - 1, 0))
    down = (gx, jnp.minimum(gy + 1, ny - 1))
    left = (jnp.maximum(gx - 1, 0), gy)
    right = (jnp.minimum(gx + 1, nx - 1), gy)
    sides = ((has_up, up), (has_down, down), (has_left, left), (has_right, right))

    def lanes_of(g):
        return pl.ds(pl.multiple_of(g * LANES, LANES), LANES)

    def remote(src, dst, send, recv, where):
        return pltpu.make_async_remote_copy(
            src_ref=src, dst_ref=dst, send_sem=send, recv_sem=recv,
            device_id=where, device_id_type=MESH,
        )

    def loads(g):
        at = lanes_of(g)
        mid = pl.ds(STRIP, OWN)
        return [
            pltpu.make_async_copy(k_hbm.at[:, at], kv.at[g, mid, pl.ds(0, LANES)], in_sem.at[g, 0]),
            pltpu.make_async_copy(v_hbm.at[:, at], kv.at[g, mid, pl.ds(LANES, LANES)], in_sem.at[g, 1]),
            pltpu.make_async_copy(q_hbm.at[:, at], q_buf.at[g], in_sem.at[g, 2]),
            pltpu.make_async_copy(g_hbm.at[:, at], g_buf.at[g], in_sem.at[g, 3]),
        ]

    def store(g, n):
        buf, hbm = ((o_buf, o_hbm), (dq_buf, dq_hbm), (dk_buf, dk_hbm), (dv_buf, dv_hbm))[n]
        return pltpu.make_async_copy(buf.at[g], hbm.at[:, lanes_of(g)], out_sem.at[g, n])

    def v_forward(g, way):
        at = lanes_of(g)
        from_rows = pl.ds(0, STRIP) if way == 0 else pl.ds(OWN - STRIP, STRIP)
        to_rows = pl.ds(STRIP + OWN, STRIP) if way == 0 else pl.ds(0, STRIP)
        return [
            remote(
                hbm.at[from_rows, at], kv.at[g, to_rows, pl.ds(n * LANES, LANES)],
                vf_send.at[g, way, n], vf_recv.at[g, way, n], up if way == 0 else down,
            )
            for n, hbm in enumerate((k_hbm, v_hbm))
        ]

    def h_forward(g, way):
        to_rows = pl.ds(CENTER + (1 - way) * SLOTS, SLOTS)
        return remote(
            hsend.at[g, pl.ds(way * SLOTS, SLOTS)], kv.at[g, to_rows],
            hf_send.at[g, way], hf_recv.at[g, way], left if way == 0 else right,
        )

    def h_return(g, way):
        return remote(
            hret_out.at[g, pl.ds(way * SLOTS, SLOTS)], hret_in.at[g, pl.ds((1 - way) * SLOTS, SLOTS)],
            hr_send.at[g, way], hr_recv.at[g, way], left if way == 0 else right,
        )

    def v_return(g, way):
        return remote(
            vret_out.at[g, way], vret_in.at[g, way],
            vr_send.at[g, way], vr_recv.at[g, way], up if way == 0 else down,
        )

    def live_v(way):
        to_rows = pl.ds(32, 16) if way == 0 else pl.ds(16, 16)
        return remote(
            dead.at[0, pl.ds(0, 16)], dead.at[0, to_rows],
            lv_send.at[way], lv_recv.at[way], up if way == 0 else down,
        )

    def live_h(way):
        return remote(
            dead.at[0, pl.ds(0, 48)], dead.at[2 - way, pl.ds(0, 48)],
            lh_send.at[way], lh_recv.at[way], left if way == 0 else right,
        )

    v_to = (has_up, has_down)
    v_from = (has_down, has_up)
    h_to = (has_left, has_right)
    h_from = (has_right, has_left)

    def start_loads(g, carry):
        for copy in loads(g):
            copy.start()
        return carry

    lax.fori_loop(0, groups, start_loads, 0)

    dead32[...] = jnp.ones_like(dead32)
    dead32[pl.ds(0, TH), pl.ds(0, TW)] = jnp.where(tissue_ref[...] > 0, 0.0, 1.0)
    dead[...] = jnp.zeros_like(dead)
    dead[0, pl.ds(0, 16), :] = dead32[...].astype(BF)
    for here, tile, first, count in (
        (has_up, 0, 16, 16), (has_down, 0, 32, 16), (has_left, 1, 0, 48), (has_right, 2, 0, 48),
    ):
        @pl.when(jnp.logical_not(here))
        def _():
            dead[tile, pl.ds(first, count), :] = jnp.ones((count, LANES), BF)

    for here, first, count in (
        (has_up, 0, STRIP), (has_down, STRIP + OWN, STRIP),
        (has_left, CENTER, SLOTS), (has_right, CENTER + SLOTS, SLOTS),
    ):
        @pl.when(jnp.logical_not(here))
        def _():
            def clear(g, carry):
                kv[g, pl.ds(first, count), :] = jnp.zeros((count, 2 * LANES), BF)
                return carry

            lax.fori_loop(0, groups, clear, 0)

    for here, way in ((has_down, 0), (has_up, 1)):
        @pl.when(jnp.logical_not(here))
        def _():
            def clear(g, carry):
                vret_in[g, way] = jnp.zeros((STRIP, 2 * LANES), BF)
                return carry

            lax.fori_loop(0, groups, clear, 0)

    for here, first in ((has_left, 0), (has_right, SLOTS)):
        @pl.when(jnp.logical_not(here))
        def _():
            def clear(g, carry):
                hret_in[g, pl.ds(first, SLOTS), :] = jnp.zeros((SLOTS, 2 * LANES), BF)
                return carry

            lax.fori_loop(0, groups, clear, 0)

    barrier = pltpu.get_barrier_semaphore()
    for here, where in sides:
        @pl.when(here)
        def _():
            pl.semaphore_signal(barrier, inc=1, device_id=where, device_id_type=MESH)
    peers = sum(here.astype(jnp.int32) for here, _ in sides)
    pl.semaphore_wait(barrier, peers)

    for way in range(2):
        @pl.when(v_to[way])
        def _():
            live_v(way).start()

    def start_forward(g, carry):
        for way in range(2):
            @pl.when(v_to[way])
            def _():
                for copy in v_forward(g, way):
                    copy.start()
        return carry

    lax.fori_loop(0, groups, start_forward, 0)

    sel[...] = select_rows((2 * SLOTS, CENTER), 0)
    sel_t[...] = select_rows((CENTER, 2 * SLOTS), 1)
    token, lane = iota((OWN, LANES), 0), iota((OWN, LANES), 1)
    same = (
        (lane < 32)
        | ((lane >= 32) & (lane < 40) & (lane - 32 == token // TW))
        | ((lane >= 40) & (lane < 72) & (lane - 40 == token % TW))
        | (lane == 72)
    )
    qfeat[...] = jnp.where(same, 1.0, 0.0).astype(BF)

    for way in range(2):
        @pl.when(v_from[way])
        def _():
            live_v(way).wait_recv()
    for way in range(2):
        @pl.when(h_to[way])
        def _():
            live_h(way).start()

    tile = dead[0].astype(F32).T.astype(BF)
    row_of, token_of = iota((LANES, OWN), 0), iota((LANES, OWN), 1)
    pick = jnp.where(row_of == token_of // TW, 1.0, 0.0).astype(BF)
    spread = jnp.dot(tile, pick, preferred_element_type=F32)
    dead_q = jnp.sum(jnp.where(row_of == token_of % TW, spread, 0.0), axis=0, keepdims=True)
    live_q[...] = jnp.broadcast_to(1.0 - dead_q, (8, OWN))

    token = iota((CENTER, LANES), 0)
    feat[pl.ds(0, CENTER), :] = key_features(
        token // TW, token % TW, token % TW, token < 0, dead[0]
    )
    for way in range(2):
        @pl.when(h_from[way])
        def _():
            live_h(way).wait_recv()
    slot = iota((SLOTS, LANES), 0)
    row = slot_row(slot)
    col = slot - row * RAD
    none = slot >= SPAN * RAD
    feat[pl.ds(CENTER, SLOTS), :] = key_features(row, col - RAD, col + TW - RAD, none, dead[1])
    feat[pl.ds(CENTER + SLOTS, SLOTS), :] = key_features(row, col + TW, col, none, dead[2])

    def send_sides(g):
        for copy in loads(g):
            copy.wait()
        for way in range(2):
            @pl.when(v_from[way])
            def _():
                for copy in v_forward(g, way):
                    copy.wait_recv()
        picked = jnp.dot(sel[...], kv[g, pl.ds(0, CENTER), :], preferred_element_type=F32)
        hsend[g] = picked.astype(BF)
        for way in range(2):
            @pl.when(h_to[way])
            def _():
                h_forward(g, way).start()

    def attend(g):
        for way in range(2):
            @pl.when(h_from[way])
            def _():
                h_forward(g, way).wait_recv()
        key_all, value_all = kv[g, :, pl.ds(0, LANES)], kv[g, :, pl.ds(LANES, LANES)]
        key_t, value_t = key_all.T, value_all.T
        query = q_buf[g] * (HD ** -0.5)
        grad = g_buf[g]
        grad_t = grad.T.astype(F32)
        with_feat = jnp.concatenate([key_all, feat[...]], axis=1)
        head_of = iota((OWN, LANES), 1) // HD
        nothing = jnp.zeros((OWN, LANES), BF)
        live_row = live_q[pl.ds(0, 1), :]
        key_grad = value_grad = None
        attended_t, query_grad_t = [], []
        contract = (((1,), (1,)), ((), ()))
        for head in range(LANES // HD):
            part = slice(head * HD, (head + 1) * HD)
            query_h = jnp.where(head_of == head, query, nothing)
            grad_h = jnp.where(head_of == head, grad, nothing)
            scores = lax.dot_general(
                with_feat, jnp.concatenate([query_h, qfeat[...]], axis=1), contract,
                preferred_element_type=F32,
            )
            top = jnp.max(scores, axis=0, keepdims=True)
            raised = jnp.exp(scores - top)
            total = jnp.sum(raised, axis=0, keepdims=True)
            attention = raised * (live_row / total)
            weight = attention.astype(BF)
            out_t = jnp.dot(value_t[part], weight, preferred_element_type=F32).astype(BF).astype(F32)
            attended_t.append(out_t)
            row_delta = jnp.sum(out_t * grad_t[part], axis=0, keepdims=True)
            grad_prob = lax.dot_general(value_all, grad_h, contract, preferred_element_type=F32)
            grad_score = (attention * (grad_prob - row_delta)).astype(BF)
            query_grad_t.append(jnp.dot(key_t[part], grad_score, preferred_element_type=F32))
            key_add = jnp.dot(grad_score, query_h, preferred_element_type=F32)
            value_add = jnp.dot(weight, grad_h, preferred_element_type=F32)
            key_grad = key_add if key_grad is None else key_grad + key_add
            value_grad = value_add if value_grad is None else value_grad + value_add
        o_buf[g] = jnp.concatenate(attended_t, axis=0).T.astype(BF)
        dq_buf[g] = (jnp.concatenate(query_grad_t, axis=0) * (HD ** -0.5)).T.astype(BF)
        store(g, 0).start()
        store(g, 1).start()
        sums = jnp.concatenate([key_grad, value_grad], axis=1)
        centre[lax.rem(g, 2)] = sums[:CENTER]
        hret_out[g] = sums[CENTER:].astype(BF)
        for way in range(2):
            @pl.when(h_to[way])
            def _():
                h_return(g, way).start()

    def send_rows(g):
        for way in range(2):
            @pl.when(h_from[way])
            def _():
                h_return(g, way).wait_recv()
        sums = centre[lax.rem(g, 2)] + jnp.dot(sel_t[...], hret_in[g], preferred_element_type=F32)
        own[g] = sums[STRIP : STRIP + OWN]
        vret_out[g, 0] = sums[:STRIP].astype(BF)
        vret_out[g, 1] = sums[STRIP + OWN :].astype(BF)
        for way in range(2):
            @pl.when(v_to[way])
            def _():
                v_return(g, way).start()

    def step(i, carry):
        @pl.when(i < groups)
        def _():
            send_sides(i)

        @pl.when((i >= 1) & (i <= groups))
        def _():
            attend(i - 1)

        @pl.when(i >= 2)
        def _():
            send_rows(i - 2)

        return carry

    lax.fori_loop(0, groups + 2, step, 0)

    def finish(g, carry):
        for way in range(2):
            @pl.when(v_from[way])
            def _():
                v_return(g, way).wait_recv()
        own[g, pl.ds(OWN - STRIP, STRIP), :] += vret_in[g, 0].astype(F32)
        own[g, pl.ds(0, STRIP), :] += vret_in[g, 1].astype(F32)
        dk_buf[g] = own[g, :, pl.ds(0, LANES)].astype(BF)
        dv_buf[g] = own[g, :, pl.ds(LANES, LANES)].astype(BF)
        store(g, 2).start()
        store(g, 3).start()
        return carry

    lax.fori_loop(0, groups, finish, 0)

    def drain(g, carry):
        for n in range(4):
            store(g, n).wait()
        for way in range(2):
            @pl.when(v_to[way])
            def _():
                for copy in v_forward(g, way):
                    copy.wait_send()
                v_return(g, way).wait_send()

            @pl.when(h_to[way])
            def _():
                h_forward(g, way).wait_send()
                h_return(g, way).wait_send()
        return carry

    lax.fori_loop(0, groups, drain, 0)
    for way in range(2):
        @pl.when(v_to[way])
        def _():
            live_v(way).wait_send()

        @pl.when(h_to[way])
        def _():
            live_h(way).wait_send()


def per_device(queries, keys, values, out_grad, tissue):
    width = queries.shape[-1]
    groups = width // LANES
    flat = (OWN, width)
    any_spec = pl.BlockSpec(memory_space=pl.ANY)
    dma = pltpu.SemaphoreType.DMA
    outs = pl.pallas_call(
        functools.partial(kernel, groups, lax.axis_size("gx"), lax.axis_size("gy")),
        out_shape=[jax.ShapeDtypeStruct(flat, BF)] * 4,
        in_specs=[any_spec] * 4 + [pl.BlockSpec(memory_space=pltpu.VMEM)],
        out_specs=[any_spec] * 4,
        scratch_shapes=[
            pltpu.VMEM((groups, KEYS, 2 * LANES), BF),
            pltpu.VMEM((groups, OWN, LANES), BF),
            pltpu.VMEM((groups, OWN, LANES), BF),
            pltpu.VMEM((KEYS, LANES), BF),
            pltpu.VMEM((OWN, LANES), BF),
            pltpu.VMEM((2 * SLOTS, CENTER), BF),
            pltpu.VMEM((CENTER, 2 * SLOTS), BF),
            pltpu.VMEM((3, LANES, LANES), BF),
            pltpu.VMEM((16, LANES), F32),
            pltpu.VMEM((8, OWN), F32),
            pltpu.VMEM((groups, 2 * SLOTS, 2 * LANES), BF),
            pltpu.VMEM((2, CENTER, 2 * LANES), F32),
            pltpu.VMEM((groups, OWN, 2 * LANES), F32),
            pltpu.VMEM((groups, 2 * SLOTS, 2 * LANES), BF),
            pltpu.VMEM((groups, 2 * SLOTS, 2 * LANES), BF),
            pltpu.VMEM((groups, 2, STRIP, 2 * LANES), BF),
            pltpu.VMEM((groups, 2, STRIP, 2 * LANES), BF),
            pltpu.VMEM((groups, OWN, LANES), BF),
            pltpu.VMEM((groups, OWN, LANES), BF),
            pltpu.VMEM((groups, OWN, LANES), BF),
            pltpu.VMEM((groups, OWN, LANES), BF),
            dma((groups, 4)), dma((groups, 4)),
            dma((groups, 2, 2)), dma((groups, 2, 2)),
            dma((groups, 2)), dma((groups, 2)),
            dma((groups, 2)), dma((groups, 2)),
            dma((groups, 2)), dma((groups, 2)),
            dma((2,)), dma((2,)), dma((2,)), dma((2,)),
        ],
        compiler_params=pltpu.CompilerParams(
            collective_id=0, has_side_effects=True, vmem_limit_bytes=56 * 1024 * 1024
        ),
    )(
        keys.reshape(flat), values.reshape(flat), queries.reshape(flat), out_grad.reshape(flat),
        tissue,
    )
    return tuple(out.reshape(queries.shape) for out in outs)


def solution(mesh):
    tokens = P("gy", "gx", None)
    return jax.shard_map(
        per_device, mesh=mesh, in_specs=(tokens,) * 4 + (P("gy", "gx"),),
        out_specs=(tokens,) * 4, check_vma=False,
    )
```

profile of v0, /device:TPU:6, one launch (start us, length us, event | category | flops | bytes accessed | tf_op | source)
XLA Modules:
  0.0 94.0 jit_solution(13199541719212996053)
XLA Ops:
  0.6 88.1 %shard_map.84 = (bf16[256,1024]{1,0:T(8,128)(2,1)}, bf16[256,1024]{1,0:T(8,128)(2,1)}, bf16[256,1024]{1,0:T(8,128)(2,1)}, bf16[256,1024]{1,0:T(8,128)(2,1)}) custom-call(bf16[256,1024]{1,0:T(8,128)(2,1)} %bitcast.12, bf16[256,1024]{1,0:T(8,128)(2,1)} %bitcast.13, bf16[256,1024]{1,0:T(8,128)(2,1)} %bitcast.14, bf16[256,1024]{1,0:T(8,128)(2,1)} %bitcast.15, ...), custom_call_target="tpu_custom_call" | custom-call | tf_op jit(solution)/shard_map/pallas_call | solution.py:413
  88.8 0.0 copy-start.2
  88.8 1.9 %copy.13 = bf16[8,32,1024]{2,1,0:T(8,128)(2,1)} copy(bf16[8,32,1024]{2,1,0:T(8,128)(2,1)} %bitcast.11) | data formatting | bytes 1048576
  90.7 0.0 copy-done.2
  90.7 0.0 copy-start.1
  90.7 0.8 copy.14
  91.5 0.4 copy-done.1
  91.9 0.0 copy-start
  91.9 0.8 copy.15
  92.7 0.4 copy-done
  93.2 0.8 copy.16
Async XLA Ops:
  88.8 1.9 %copy-start.2 = (bf16[256,1024]{1,0:T(8,128)(2,1)S(1)}, bf16[256,1024]{1,0:T(8,128)(2,1)}, u32[]{:S(2)}) copy-start(bf16[256,1024]{1,0:T(8,128)(2,1)} %get-tuple-element.9) | copy-start | bytes 1572868
  90.7 1.2 %copy-start.1 = (bf16[256,1024]{1,0:T(8,128)(2,1)S(1)}, bf16[256,1024]{1,0:T(8,128)(2,1)}, u32[]{:S(2)}) copy-start(bf16[256,1024]{1,0:T(8,128)(2,1)} %get-tuple-element.10) | copy-start | bytes 1572868
  91.9 1.2 %copy-start = (bf16[256,1024]{1,0:T(8,128)(2,1)S(1)}, bf16[256,1024]{1,0:T(8,128)(2,1)}, u32[]{:S(2)}) copy-start(bf16[256,1024]{1,0:T(8,128)(2,1)} %get-tuple-element.11) | copy-start | bytes 1572868
where the time goes:
time: 95 us; the launch traced here: 94 us
  Pallas kernels  88.1 us (93%)
  local copies, waits for them, and re-layouts  5.18 us (5%)
    pallas_call x1, Pallas kernels, per_device(): pl.pallas_call(functools.partial(kernel, groups, lax.axis_size('gx'), lax...  88.1 us
    unnamed x10, local copies, waits for them, and re-layouts  5.18 us

commit v1 on v0

--- a/solution.py
+++ b/solution.py
@@ -20,6 +20,8 @@
 SLOTS = 128
 KEYS = CENTER + 2 * SLOTS
 FAR = -1e30
+LEAD = 3
+RATE = 1
 BF = jnp.bfloat16
 F32 = jnp.float32
 
@@ -67,8 +69,10 @@
     kv, q_buf, g_buf, feat, qfeat, sel, sel_t, dead, dead32, live_q,
     hsend, centre, own, hret_out, hret_in, vret_out, vret_in,
     o_buf, dq_buf, dk_buf, dv_buf,
+    row_relay, row_relay_back, side_relay, side_relay_back,
     in_sem, out_sem, vf_send, vf_recv, hf_send, hf_recv, hr_send, hr_recv, vr_send, vr_recv,
     lv_send, lv_recv, lh_send, lh_recv,
+    rf_send, rf_recv, rb_send, rb_recv, sf_send, sf_recv, sb_send, sb_recv,
 ):
     gx, gy = lax.axis_index("gx"), lax.axis_index("gy")
     has_up, has_down = gy > 0, gy < ny - 1
@@ -77,7 +81,58 @@
     down = (gx, jnp.minimum(gy + 1, ny - 1))
     left = (jnp.maximum(gx - 1, 0), gy)
     right = (jnp.minimum(gx + 1, nx - 1), gy)
-    sides = ((has_up, up), (has_down, down), (has_left, left), (has_right, right))
+    two_up = (gx, jnp.maximum(gy - 2, 0))
+    two_down = (gx, jnp.minimum(gy + 2, ny - 1))
+
+    def picked(g, count):
+        inner = (g >= 1) & (g <= 6)
+        even = lax.rem(g, 2) == 0
+        half = ((g < 4) & jnp.logical_not(even)) | ((g >= 4) & even)
+        return (
+            ((count == 6) & inner) | ((count == 4) & inner & half) | ((count == 2) & ((g == 2) | (g == 5)))
+        )
+
+    even_row = lax.rem(gy, 2) == 0
+    relayed_count = (jnp.where(even_row, gy, 0), jnp.where(even_row, 0, ny - 1 - gy))
+    relay_for = (down, up)
+    hand_count = jnp.where(even_row, ny - 2 - gy, gy - 1)
+
+    def by_relay(g, way):
+        return picked(g, relayed_count[way])
+
+    def hands_on(g):
+        return picked(g, hand_count)
+
+    half = nx // 2
+    seam = (gx == half - 1) | (gx == half)
+    at_seam = ((gx == half), (gx == half - 1))
+    routes = 3
+    by_way = (tuple(2 * n for n in range(routes)), tuple(nx - 1 - 2 * n for n in range(routes)))
+
+    def side_route(g):
+        return jnp.where((g >= 1) & (g <= 6), 1 + lax.rem(g - 1, routes), 0)
+
+    def relay_of(g, way):
+        number = jnp.maximum(side_route(g) - 1, 0)
+        return (2 * number if way == 0 else nx - 1 - 2 * number, gy)
+
+    def side_picked(g):
+        return side_route(g) > 0
+
+    def hands_sides(g, way):
+        return side_picked(g) & (gx == relay_of(g, way)[0])
+
+    seam_to = ((half - 1, gy), (half, gy))
+    on_route = (gx == by_way[0][0])
+    for spot in by_way[0][1:] + by_way[1]:
+        on_route = on_route | (gx == spot)
+
+    sides = [
+        (has_up, up), (has_down, down), (has_left, left), (has_right, right),
+        (gy >= 2, two_up), (gy < ny - 2, two_down),
+    ]
+    sides += [(seam, (spot, gy)) for spot in by_way[0] + by_way[1]]
+    sides += [(on_route, spot) for spot in seam_to]
 
     def lanes_of(g):
         return pl.ds(pl.multiple_of(g * LANES, LANES), LANES)
@@ -114,6 +169,63 @@
             for n, hbm in enumerate((k_hbm, v_hbm))
         ]
 
+    def v_forward_first(g, way):
+        at = lanes_of(g)
+        from_rows = pl.ds(0, STRIP) if way == 0 else pl.ds(OWN - STRIP, STRIP)
+        return [
+            remote(
+                hbm.at[from_rows, at], row_relay.at[g, :, pl.ds(n * LANES, LANES)],
+                vf_send.at[g, way, n], rf_recv.at[g, n], relay_for[way],
+            )
+            for n, hbm in enumerate((k_hbm, v_hbm))
+        ]
+
+    def v_forward_second(g, way):
+        to_rows = pl.ds(STRIP + OWN, STRIP) if way == 0 else pl.ds(0, STRIP)
+        return [
+            remote(
+                row_relay.at[g, :, pl.ds(n * LANES, LANES)], kv.at[g, to_rows, pl.ds(n * LANES, LANES)],
+                rf_send.at[g, n], vf_recv.at[g, way, n], two_up if way == 0 else two_down,
+            )
+            for n in range(2)
+        ]
+
+    def v_return_first(g, way):
+        return remote(
+            vret_out.at[g, way], row_relay_back.at[g],
+            vr_send.at[g, way], rb_recv.at[g], relay_for[way],
+        )
+
+    def v_return_second(g, way):
+        return remote(
+            row_relay_back.at[g], vret_in.at[g, way],
+            rb_send.at[g], vr_recv.at[g, way], two_up if way == 0 else two_down,
+        )
+
+    def h_forward_first(g, way):
+        return remote(
+            hsend.at[g, pl.ds(way * SLOTS, SLOTS)], side_relay.at[g],
+            hf_send.at[g, way], sf_recv.at[g], relay_of(g, way),
+        )
+
+    def h_forward_second(g, way):
+        to_rows = pl.ds(CENTER + (1 - way) * SLOTS, SLOTS)
+        return remote(
+            side_relay.at[g], kv.at[g, to_rows], sf_send.at[g], hf_recv.at[g, way], seam_to[way],
+        )
+
+    def h_return_first(g, way):
+        return remote(
+            hret_out.at[g, pl.ds(way * SLOTS, SLOTS)], side_relay_back.at[g],
+            hr_send.at[g, way], sb_recv.at[g], relay_of(g, way),
+        )
+
+    def h_return_second(g, way):
+        return remote(
+            side_relay_back.at[g], hret_in.at[g, pl.ds((1 - way) * SLOTS, SLOTS)],
+            sb_send.at[g], hr_recv.at[g, way], seam_to[way],
+        )
+
     def h_forward(g, way):
         to_rows = pl.ds(CENTER + (1 - way) * SLOTS, SLOTS)
         return remote(
@@ -150,6 +262,24 @@
     v_from = (has_down, has_up)
     h_to = (has_left, has_right)
     h_from = (has_right, has_left)
+
+    def send(here, special, direct, first):
+        @pl.when(here & jnp.logical_not(special))
+        def _():
+            for copy in direct():
+                copy.start()
+
+        @pl.when(here & special)
+        def _():
+            for copy in first():
+                copy.start()
+
+    def start_rows(g):
+        for way in range(2):
+            send(
+                v_to[way], by_relay(g, way),
+                lambda: v_forward(g, way), lambda: v_forward_first(g, way),
+            )
 
     def start_loads(g, carry):
         for copy in loads(g):
@@ -213,14 +343,10 @@
             live_v(way).start()
 
     def start_forward(g, carry):
-        for way in range(2):
-            @pl.when(v_to[way])
-            def _():
-                for copy in v_forward(g, way):
-                    copy.start()
+        start_rows(g)
         return carry
 
-    lax.fori_loop(0, groups, start_forward, 0)
+    lax.fori_loop(0, LEAD, start_forward, 0)
 
     sel[...] = select_rows((2 * SLOTS, CENTER), 0)
     sel_t[...] = select_rows((CENTER, 2 * SLOTS), 1)
@@ -275,9 +401,10 @@
         picked = jnp.dot(sel[...], kv[g, pl.ds(0, CENTER), :], preferred_element_type=F32)
         hsend[g] = picked.astype(BF)
         for way in range(2):
-            @pl.when(h_to[way])
-            def _():
-                h_forward(g, way).start()
+            send(
+                h_to[way], at_seam[way] & side_picked(g),
+                lambda: [h_forward(g, way)], lambda: [h_forward_first(g, way)],
+            )
 
     def attend(g):
         for way in range(2):
@@ -324,43 +451,81 @@
         store(g, 0).start()
         store(g, 1).start()
         sums = jnp.concatenate([key_grad, value_grad], axis=1)
-        centre[lax.rem(g, 2)] = sums[:CENTER]
+        centre[lax.rem(g, 3)] = sums[:CENTER]
         hret_out[g] = sums[CENTER:].astype(BF)
         for way in range(2):
-            @pl.when(h_to[way])
-            def _():
-                h_return(g, way).start()
+            send(
+                h_to[way], at_seam[way] & side_picked(g),
+                lambda: [h_return(g, way)], lambda: [h_return_first(g, way)],
+            )
 
     def send_rows(g):
         for way in range(2):
             @pl.when(h_from[way])
             def _():
                 h_return(g, way).wait_recv()
-        sums = centre[lax.rem(g, 2)] + jnp.dot(sel_t[...], hret_in[g], preferred_element_type=F32)
+        sums = centre[lax.rem(g, 3)] + jnp.dot(sel_t[...], hret_in[g], preferred_element_type=F32)
         own[g] = sums[STRIP : STRIP + OWN]
         vret_out[g, 0] = sums[:STRIP].astype(BF)
         vret_out[g, 1] = sums[STRIP + OWN :].astype(BF)
         for way in range(2):
-            @pl.when(v_to[way])
-            def _():
-                v_return(g, way).start()
+            send(
+                v_to[way], by_relay(g, way),
+                lambda: [v_return(g, way)], lambda: [v_return_first(g, way)],
+            )
+
+    def hand_rows(g):
+        for way, mine in ((0, jnp.logical_not(even_row)), (1, even_row)):
+            @pl.when(mine & hands_on(g))
+            def _():
+                for copy in v_forward_first(g, way):
+                    copy.wait_recv()
+                for copy in v_forward_second(g, way):
+                    copy.start()
+
+    def hand_rows_back(g):
+        for way, mine in ((0, jnp.logical_not(even_row)), (1, even_row)):
+            @pl.when(mine & hands_on(g))
+            def _():
+                v_return_first(g, way).wait_recv()
+                v_return_second(g, way).start()
+
+    def hand_sides(g):
+        for way in range(2):
+            @pl.when(hands_sides(g, way))
+            def _():
+                h_forward_first(g, way).wait_recv()
+                h_forward_second(g, way).start()
+
+    def hand_sides_back(g):
+        for way in range(2):
+            @pl.when(hands_sides(g, way))
+            def _():
+                h_return_first(g, way).wait_recv()
+                h_return_second(g, way).start()
 
     def step(i, carry):
-        @pl.when(i < groups)
-        def _():
-            send_sides(i)
-
-        @pl.when((i >= 1) & (i <= groups))
-        def _():
-            attend(i - 1)
-
-        @pl.when(i >= 2)
-        def _():
-            send_rows(i - 2)
-
+        def stage(lag, work):
+            @pl.when((i >= lag) & (i < groups + lag))
+            def _():
+                work(i - lag)
+
+        for n in range(RATE):
+            @pl.when(LEAD + RATE * i + n < groups)
+            def _():
+                start_rows(LEAD + RATE * i + n)
+
+        stage(-1, hand_rows)
+        stage(1, hand_sides)
+        stage(0, send_sides)
+        stage(3, attend)
+        stage(4, hand_sides_back)
+        stage(5, send_rows)
+        stage(6, hand_rows_back)
         return carry
 
-    lax.fori_loop(0, groups + 2, step, 0)
+    hand_rows(0)
+    lax.fori_loop(0, groups + 6, step, 0)
 
     def finish(g, carry):
         for way in range(2):
@@ -391,6 +556,18 @@
             def _():
                 h_forward(g, way).wait_send()
                 h_return(g, way).wait_send()
+
+        @pl.when(hands_on(g))
+        def _():
+            for copy in v_forward_second(g, 0):
+                copy.wait_send()
+            v_return_second(g, 0).wait_send()
+
+        @pl.when(hands_sides(g, 0) | hands_sides(g, 1))
+        def _():
+            h_forward_second(g, 0).wait_send()
+            h_return_second(g, 0).wait_send()
+
         return carry
 
     lax.fori_loop(0, groups, drain, 0)
@@ -402,6 +579,19 @@
         @pl.when(h_to[way])
         def _():
             live_h(way).wait_send()
+
+
+def write_out(*refs):
+    ins, outs, bufs, sem = refs[:4], refs[4:8], refs[8:12], refs[12]
+    reads = [pltpu.make_async_copy(a, b, sem.at[0, n]) for n, (a, b) in enumerate(zip(ins, bufs))]
+    writes = [pltpu.make_async_copy(a, b, sem.at[1, n]) for n, (a, b) in enumerate(zip(bufs, outs))]
+    for copy in reads:
+        copy.start()
+    for read, write in zip(reads, writes):
+        read.wait()
+        write.start()
+    for copy in writes:
+        copy.wait()
 
 
 def per_device(queries, keys, values, out_grad, tissue):
@@ -427,7 +617,7 @@
             pltpu.VMEM((16, LANES), F32),
             pltpu.VMEM((8, OWN), F32),
             pltpu.VMEM((groups, 2 * SLOTS, 2 * LANES), BF),
-            pltpu.VMEM((2, CENTER, 2 * LANES), F32),
+            pltpu.VMEM((3, CENTER, 2 * LANES), F32),
             pltpu.VMEM((groups, OWN, 2 * LANES), F32),
             pltpu.VMEM((groups, 2 * SLOTS, 2 * LANES), BF),
             pltpu.VMEM((groups, 2 * SLOTS, 2 * LANES), BF),
@@ -437,12 +627,18 @@
             pltpu.VMEM((groups, OWN, LANES), BF),
             pltpu.VMEM((groups, OWN, LANES), BF),
             pltpu.VMEM((groups, OWN, LANES), BF),
+            pltpu.VMEM((groups, STRIP, 2 * LANES), BF),
+            pltpu.VMEM((groups, STRIP, 2 * LANES), BF),
+            pltpu.VMEM((groups, SLOTS, 2 * LANES), BF),
+            pltpu.VMEM((groups, SLOTS, 2 * LANES), BF),
             dma((groups, 4)), dma((groups, 4)),
             dma((groups, 2, 2)), dma((groups, 2, 2)),
             dma((groups, 2)), dma((groups, 2)),
             dma((groups, 2)), dma((groups, 2)),
             dma((groups, 2)), dma((groups, 2)),
             dma((2,)), dma((2,)), dma((2,)), dma((2,)),
+            dma((groups, 2)), dma((groups, 2)), dma((groups,)), dma((groups,)),
+            dma((groups,)), dma((groups,)), dma((groups,)), dma((groups,)),
         ],
         compiler_params=pltpu.CompilerParams(
             collective_id=0, has_side_effects=True, vmem_limit_bytes=56 * 1024 * 1024
@@ -451,6 +647,13 @@
         keys.reshape(flat), values.reshape(flat), queries.reshape(flat), out_grad.reshape(flat),
         tissue,
     )
+    outs = pl.pallas_call(
+        write_out,
+        out_shape=[jax.ShapeDtypeStruct(flat, BF)] * 4,
+        in_specs=[any_spec] * 4,
+        out_specs=[any_spec] * 4,
+        scratch_shapes=[pltpu.VMEM(flat, BF)] * 4 + [dma((2, 4))],
+    )(*outs)
     return tuple(out.reshape(queries.shape) for out in outs)
 
 

time: 95 us -> 83.7 us (0.88)
  Pallas kernels: 88.1 us -> 81.5 us
  local copies, waits for them, and re-layouts: 5.18 us -> 0 us
    pallas_call x1, Pallas kernels: 88.1 us -> 79 us  [per_device(): pl.pallas_call(functools.partial(kernel, groups, lax.axis_size('gx'), lax...]
    unnamed x10 -> x0, local copies, waits for them, and re-layouts: 5.18 us -> none
    pallas_call x0 -> x1, Pallas kernels: none -> 2.42 us  [per_device(): pl.pallas_call(write_out, out_shape=[jax.ShapeDtypeStruct(flat, BF)] * 4,...]
where the time goes in v1:
time: 83.7 us; the launch traced here: 82.1 us
  Pallas kernels  81.5 us (97%)
    pallas_call x1, Pallas kernels, per_device(): pl.pallas_call(functools.partial(kernel, groups, lax.axis_size('gx'), lax...  79 us
    pallas_call x1, Pallas kernels, per_device(): pl.pallas_call(write_out, out_shape=[jax.ShapeDtypeStruct(flat, BF)] * 4,...  2.42 us

profile of v1, /device:TPU:6, one launch (start us, length us, event | category | flops | bytes accessed | tf_op | source)
XLA Modules:
  0.0 82.1 jit_solution(12386129536447103529)
XLA Ops:
  0.6 79.0 %shard_map.84 = (bf16[256,1024]{1,0:T(8,128)(2,1)}, bf16[256,1024]{1,0:T(8,128)(2,1)}, bf16[256,1024]{1,0:T(8,128)(2,1)}, bf16[256,1024]{1,0:T(8,128)(2,1)}) custom-call(bf16[256,1024]{1,0:T(8,128)(2,1)} %bitcast.8, bf16[256,1024]{1,0:T(8,128)(2,1)} %bitcast.9, bf16[256,1024]{1,0:T(8,128)(2,1)} %bitcast.10, bf16[256,1024]{1,0:T(8,128)(2,1)} %bitcast.11, ...), custom_call_target="tpu_custom_call" | custom-call | tf_op jit(solution)/shard_map/pallas_call | solution.py:603
  79.7 2.4 %shard_map.85 = (bf16[256,1024]{1,0:T(8,128)(2,1)}, bf16[256,1024]{1,0:T(8,128)(2,1)}, bf16[256,1024]{1,0:T(8,128)(2,1)}, bf16[256,1024]{1,0:T(8,128)(2,1)}) custom-call(bf16[256,1024]{1,0:T(8,128)(2,1)} %get-tuple-element.12.refs_0_, bf16[256,1024]{1,0:T(8,128)(2,1)} %get-tuple-element.13.refs_1_, bf16[256,1024]{1,0:T(8,128)(2,1)} %get-tuple-element.14.refs_2_, ...), custom_call_target="tpu_custom_call" | custom-call | tf_op jit(solution)/shard_map/pallas_call | solution.py:650

commit v2 on v1

--- a/solution.py
+++ b/solution.py
@@ -19,6 +19,9 @@
 SPAN = TH + 2 * RAD
 SLOTS = 128
 KEYS = CENTER + 2 * SLOTS
+TOP = OWN - STRIP
+SIDES = 3 * OWN
+ROWS = SIDES + 2 * SLOTS
 FAR = -1e30
 LEAD = 3
 RATE = 1
@@ -67,12 +70,13 @@
     k_hbm, v_hbm, q_hbm, g_hbm, tissue_ref,
     o_hbm, dq_hbm, dk_hbm, dv_hbm,
     kv, q_buf, g_buf, feat, qfeat, sel, sel_t, dead, dead32, live_q,
-    hsend, centre, own, hret_out, hret_in, vret_out, vret_in,
+    hsend, centre, own, part, hret_out, hret_in, xret_out, xret_in, zret_out, zret_in,
     o_buf, dq_buf, dk_buf, dv_buf,
-    row_relay, row_relay_back, side_relay, side_relay_back,
-    in_sem, out_sem, vf_send, vf_recv, hf_send, hf_recv, hr_send, hr_recv, vr_send, vr_recv,
+    side_relay, side_relay_back,
+    in_sem, out_sem, zf_send, zf_recv, xf_send, xf_recv, hf_send, hf_recv, hr_send, hr_recv,
+    xr_send, xr_recv, zr_send, zr_recv,
     lv_send, lv_recv, lh_send, lh_recv,
-    rf_send, rf_recv, rb_send, rb_recv, sf_send, sf_recv, sb_send, sb_recv,
+    sf_send, sf_recv, sb_send, sb_recv,
 ):
     gx, gy = lax.axis_index("gx"), lax.axis_index("gy")
     has_up, has_down = gy > 0, gy < ny - 1
@@ -81,27 +85,13 @@
     down = (gx, jnp.minimum(gy + 1, ny - 1))
     left = (jnp.maximum(gx - 1, 0), gy)
     right = (jnp.minimum(gx + 1, nx - 1), gy)
-    two_up = (gx, jnp.maximum(gy - 2, 0))
-    two_down = (gx, jnp.minimum(gy + 2, ny - 1))
-
-    def picked(g, count):
-        inner = (g >= 1) & (g <= 6)
-        even = lax.rem(g, 2) == 0
-        half = ((g < 4) & jnp.logical_not(even)) | ((g >= 4) & even)
-        return (
-            ((count == 6) & inner) | ((count == 4) & inner & half) | ((count == 2) & ((g == 2) | (g == 5)))
-        )
-
-    even_row = lax.rem(gy, 2) == 0
-    relayed_count = (jnp.where(even_row, gy, 0), jnp.where(even_row, 0, ny - 1 - gy))
-    relay_for = (down, up)
-    hand_count = jnp.where(even_row, ny - 2 - gy, gy - 1)
-
-    def by_relay(g, way):
-        return picked(g, relayed_count[way])
-
-    def hands_on(g):
-        return picked(g, hand_count)
+    odd = lax.rem(gy, 2)
+    even_row = odd == 0
+    partner = (gx, gy + 1 - 2 * odd)
+    has_next = jnp.where(even_row, gy < ny - 2, gy >= 2)
+    has_last = jnp.where(even_row, gy >= 2, gy < ny - 2)
+    next_tile = (gx, jnp.clip(gy + 2 - 4 * odd, 0, ny - 1))
+    last_tile = (gx, jnp.clip(gy - 2 + 4 * odd, 0, ny - 1))
 
     half = nx // 2
     seam = (gx == half - 1) | (gx == half)
@@ -129,7 +119,7 @@
 
     sides = [
         (has_up, up), (has_down, down), (has_left, left), (has_right, right),
-        (gy >= 2, two_up), (gy < ny - 2, two_down),
+        (has_next, next_tile), (has_last, last_tile),
     ]
     sides += [(seam, (spot, gy)) for spot in by_way[0] + by_way[1]]
     sides += [(on_route, spot) for spot in seam_to]
@@ -145,7 +135,7 @@
 
     def loads(g):
         at = lanes_of(g)
-        mid = pl.ds(STRIP, OWN)
+        mid = pl.ds(OWN, OWN)
         return [
             pltpu.make_async_copy(k_hbm.at[:, at], kv.at[g, mid, pl.ds(0, LANES)], in_sem.at[g, 0]),
             pltpu.make_async_copy(v_hbm.at[:, at], kv.at[g, mid, pl.ds(LANES, LANES)], in_sem.at[g, 1]),
@@ -157,50 +147,26 @@
         buf, hbm = ((o_buf, o_hbm), (dq_buf, dq_hbm), (dk_buf, dk_hbm), (dv_buf, dv_hbm))[n]
         return pltpu.make_async_copy(buf.at[g], hbm.at[:, lanes_of(g)], out_sem.at[g, n])
 
-    def v_forward(g, way):
-        at = lanes_of(g)
-        from_rows = pl.ds(0, STRIP) if way == 0 else pl.ds(OWN - STRIP, STRIP)
-        to_rows = pl.ds(STRIP + OWN, STRIP) if way == 0 else pl.ds(0, STRIP)
+    def z_forward(g):
+        to_rows = pl.ds(pl.multiple_of(odd * (2 * OWN), OWN), OWN)
         return [
             remote(
-                hbm.at[from_rows, at], kv.at[g, to_rows, pl.ds(n * LANES, LANES)],
-                vf_send.at[g, way, n], vf_recv.at[g, way, n], up if way == 0 else down,
+                hbm.at[:, lanes_of(g)], kv.at[g, to_rows, pl.ds(n * LANES, LANES)],
+                zf_send.at[g, n], zf_recv.at[g, n], partner,
             )
             for n, hbm in enumerate((k_hbm, v_hbm))
         ]
 
-    def v_forward_first(g, way):
-        at = lanes_of(g)
-        from_rows = pl.ds(0, STRIP) if way == 0 else pl.ds(OWN - STRIP, STRIP)
-        return [
-            remote(
-                hbm.at[from_rows, at], row_relay.at[g, :, pl.ds(n * LANES, LANES)],
-                vf_send.at[g, way, n], rf_recv.at[g, n], relay_for[way],
-            )
-            for n, hbm in enumerate((k_hbm, v_hbm))
-        ]
-
-    def v_forward_second(g, way):
-        to_rows = pl.ds(STRIP + OWN, STRIP) if way == 0 else pl.ds(0, STRIP)
-        return [
-            remote(
-                row_relay.at[g, :, pl.ds(n * LANES, LANES)], kv.at[g, to_rows, pl.ds(n * LANES, LANES)],
-                rf_send.at[g, n], vf_recv.at[g, way, n], two_up if way == 0 else two_down,
-            )
-            for n in range(2)
-        ]
-
-    def v_return_first(g, way):
-        return remote(
-            vret_out.at[g, way], row_relay_back.at[g],
-            vr_send.at[g, way], rb_recv.at[g], relay_for[way],
-        )
-
-    def v_return_second(g, way):
-        return remote(
-            row_relay_back.at[g], vret_in.at[g, way],
-            rb_send.at[g], vr_recv.at[g, way], two_up if way == 0 else two_down,
-        )
+    def x_forward(g):
+        from_rows = pl.ds(pl.multiple_of((1 - odd) * (SIDES - STRIP), 64), STRIP)
+        to_rows = pl.ds(pl.multiple_of(TOP + odd * (STRIP + OWN), 64), STRIP)
+        return remote(kv.at[g, from_rows], kv.at[g, to_rows], xf_send.at[g], xf_recv.at[g], next_tile)
+
+    def x_return(g):
+        return remote(xret_out.at[g], xret_in.at[g], xr_send.at[g], xr_recv.at[g], last_tile)
+
+    def z_return(g):
+        return remote(zret_out.at[g], zret_in.at[g], zr_send.at[g], zr_recv.at[g], partner)
 
     def h_forward_first(g, way):
         return remote(
@@ -209,7 +175,7 @@
         )
 
     def h_forward_second(g, way):
-        to_rows = pl.ds(CENTER + (1 - way) * SLOTS, SLOTS)
+        to_rows = pl.ds(SIDES + (1 - way) * SLOTS, SLOTS)
         return remote(
             side_relay.at[g], kv.at[g, to_rows], sf_send.at[g], hf_recv.at[g, way], seam_to[way],
         )
@@ -227,7 +193,7 @@
         )
 
     def h_forward(g, way):
-        to_rows = pl.ds(CENTER + (1 - way) * SLOTS, SLOTS)
+        to_rows = pl.ds(SIDES + (1 - way) * SLOTS, SLOTS)
         return remote(
             hsend.at[g, pl.ds(way * SLOTS, SLOTS)], kv.at[g, to_rows],
             hf_send.at[g, way], hf_recv.at[g, way], left if way == 0 else right,
@@ -237,12 +203,6 @@
         return remote(
             hret_out.at[g, pl.ds(way * SLOTS, SLOTS)], hret_in.at[g, pl.ds((1 - way) * SLOTS, SLOTS)],
             hr_send.at[g, way], hr_recv.at[g, way], left if way == 0 else right,
-        )
-
-    def v_return(g, way):
-        return remote(
-            vret_out.at[g, way], vret_in.at[g, way],
-            vr_send.at[g, way], vr_recv.at[g, way], up if way == 0 else down,
         )
 
     def live_v(way):
@@ -275,11 +235,8 @@
                 copy.start()
 
     def start_rows(g):
-        for way in range(2):
-            send(
-                v_to[way], by_relay(g, way),
-                lambda: v_forward(g, way), lambda: v_forward_first(g, way),
-            )
+        for copy in z_forward(g):
+            copy.start()
 
     def start_loads(g, carry):
         for copy in loads(g):
@@ -300,8 +257,8 @@
             dead[tile, pl.ds(first, count), :] = jnp.ones((count, LANES), BF)
 
     for here, first, count in (
-        (has_up, 0, STRIP), (has_down, STRIP + OWN, STRIP),
-        (has_left, CENTER, SLOTS), (has_right, CENTER + SLOTS, SLOTS),
+        (has_up, TOP, STRIP), (has_down, 2 * OWN, STRIP),
+        (has_left, SIDES, SLOTS), (has_right, SIDES + SLOTS, SLOTS),
     ):
         @pl.when(jnp.logical_not(here))
         def _():
@@ -311,14 +268,13 @@
 
             lax.fori_loop(0, groups, clear, 0)
 
-    for here, way in ((has_down, 0), (has_up, 1)):
-        @pl.when(jnp.logical_not(here))
-        def _():
-            def clear(g, carry):
-                vret_in[g, way] = jnp.zeros((STRIP, 2 * LANES), BF)
-                return carry
-
-            lax.fori_loop(0, groups, clear, 0)
+    @pl.when(jnp.logical_not(has_next))
+    def _():
+        def clear(g, carry):
+            xret_in[g] = jnp.zeros((STRIP, 2 * LANES), BF)
+            return carry
+
+        lax.fori_loop(0, groups, clear, 0)
 
     for here, first in ((has_left, 0), (has_right, SLOTS)):
         @pl.when(jnp.logical_not(here))
@@ -393,12 +349,12 @@
     def send_sides(g):
         for copy in loads(g):
             copy.wait()
-        for way in range(2):
-            @pl.when(v_from[way])
-            def _():
-                for copy in v_forward(g, way):
-                    copy.wait_recv()
-        picked = jnp.dot(sel[...], kv[g, pl.ds(0, CENTER), :], preferred_element_type=F32)
+
+        @pl.when(has_last)
+        def _():
+            x_forward(g).wait_recv()
+
+        picked = jnp.dot(sel[...], kv[g, pl.ds(TOP, CENTER), :], preferred_element_type=F32)
         hsend[g] = picked.astype(BF)
         for way in range(2):
             send(
@@ -411,7 +367,13 @@
             @pl.when(h_from[way])
             def _():
                 h_forward(g, way).wait_recv()
-        key_all, value_all = kv[g, :, pl.ds(0, LANES)], kv[g, :, pl.ds(LANES, LANES)]
+        key_all, value_all = (
+            jnp.concatenate(
+                [kv[g, pl.ds(TOP, CENTER), pl.ds(n, LANES)], kv[g, pl.ds(SIDES, 2 * SLOTS), pl.ds(n, LANES)]],
+                axis=0,
+            )
+            for n in (0, LANES)
+        )
         key_t, value_t = key_all.T, value_all.T
         query = q_buf[g] * (HD ** -0.5)
         grad = g_buf[g]
@@ -420,34 +382,61 @@
         head_of = iota((OWN, LANES), 1) // HD
         nothing = jnp.zeros((OWN, LANES), BF)
         live_row = live_q[pl.ds(0, 1), :]
-        key_grad = value_grad = None
-        attended_t, query_grad_t = [], []
         contract = (((1,), (1,)), ((), ()))
-        for head in range(LANES // HD):
-            part = slice(head * HD, (head + 1) * HD)
-            query_h = jnp.where(head_of == head, query, nothing)
-            grad_h = jnp.where(head_of == head, grad, nothing)
-            scores = lax.dot_general(
-                with_feat, jnp.concatenate([query_h, qfeat[...]], axis=1), contract,
+        parts = [slice(head * HD, (head + 1) * HD) for head in range(2)]
+        queries_h = [jnp.where(head_of == head, query, nothing) for head in range(2)]
+        grads_h = [jnp.where(head_of == head, grad, nothing) for head in range(2)]
+
+        def scores_of(head):
+            return lax.dot_general(
+                with_feat, jnp.concatenate([queries_h[head], qfeat[...]], axis=1), contract,
                 preferred_element_type=F32,
             )
+
+        def attention_of(scores):
             top = jnp.max(scores, axis=0, keepdims=True)
             raised = jnp.exp(scores - top)
             total = jnp.sum(raised, axis=0, keepdims=True)
-            attention = raised * (live_row / total)
-            weight = attention.astype(BF)
-            out_t = jnp.dot(value_t[part], weight, preferred_element_type=F32).astype(BF).astype(F32)
-            attended_t.append(out_t)
-            row_delta = jnp.sum(out_t * grad_t[part], axis=0, keepdims=True)
-            grad_prob = lax.dot_general(value_all, grad_h, contract, preferred_element_type=F32)
-            grad_score = (attention * (grad_prob - row_delta)).astype(BF)
-            query_grad_t.append(jnp.dot(key_t[part], grad_score, preferred_element_type=F32))
-            key_add = jnp.dot(grad_score, query_h, preferred_element_type=F32)
-            value_add = jnp.dot(weight, grad_h, preferred_element_type=F32)
-            key_grad = key_add if key_grad is None else key_grad + key_add
-            value_grad = value_add if value_grad is None else value_grad + value_add
-        o_buf[g] = jnp.concatenate(attended_t, axis=0).T.astype(BF)
-        dq_buf[g] = (jnp.concatenate(query_grad_t, axis=0) * (HD ** -0.5)).T.astype(BF)
+            return raised * (live_row / total)
+
+        def attended_of(head, weight):
+            out = jnp.dot(value_t[parts[head]], weight, preferred_element_type=F32)
+            return out.astype(BF).astype(F32)
+
+        def delta_of(head, out):
+            return jnp.sum(out * grad_t[parts[head]], axis=0, keepdims=True)
+
+        def grad_prob_of(head):
+            return lax.dot_general(value_all, grads_h[head], contract, preferred_element_type=F32)
+
+        def query_grad_of(head, grad_score):
+            return jnp.dot(key_t[parts[head]], grad_score, preferred_element_type=F32)
+
+        scores_0, scores_1 = scores_of(0), scores_of(1)
+        attention_0 = attention_of(scores_0)
+        weight_0 = attention_0.astype(BF)
+        prob_0 = grad_prob_of(0)
+        out_0 = attended_of(0, weight_0)
+        attention_1 = attention_of(scores_1)
+        weight_1 = attention_1.astype(BF)
+        prob_1 = grad_prob_of(1)
+        delta_0 = delta_of(0, out_0)
+        out_1 = attended_of(1, weight_1)
+        score_0 = (attention_0 * (prob_0 - delta_0)).astype(BF)
+        delta_1 = delta_of(1, out_1)
+        query_grad_0 = query_grad_of(0, score_0)
+        score_1 = (attention_1 * (prob_1 - delta_1)).astype(BF)
+        query_grad_1 = query_grad_of(1, score_1)
+        key_grad = jnp.dot(
+            jnp.concatenate([score_0, score_1], axis=1), jnp.concatenate(queries_h, axis=0),
+            preferred_element_type=F32,
+        )
+        value_grad = jnp.dot(
+            jnp.concatenate([weight_0, weight_1], axis=1), jnp.concatenate(grads_h, axis=0),
+            preferred_element_type=F32,
+        )
+        o_buf[g] = jnp.concatenate([out_0, out_1], axis=0).T.astype(BF)
+        dq_buf[g] = (jnp.concatenate([query_grad_0, query_grad_1], axis=0) * (HD ** -0.5)).T.astype(BF)
         store(g, 0).start()
         store(g, 1).start()
         sums = jnp.concatenate([key_grad, value_grad], axis=1)
@@ -466,29 +455,42 @@
                 h_return(g, way).wait_recv()
         sums = centre[lax.rem(g, 3)] + jnp.dot(sel_t[...], hret_in[g], preferred_element_type=F32)
         own[g] = sums[STRIP : STRIP + OWN]
-        vret_out[g, 0] = sums[:STRIP].astype(BF)
-        vret_out[g, 1] = sums[STRIP + OWN :].astype(BF)
-        for way in range(2):
-            send(
-                v_to[way], by_relay(g, way),
-                lambda: [v_return(g, way)], lambda: [v_return_first(g, way)],
-            )
+        above, below = sums[:STRIP], sums[STRIP + OWN :]
+
+        @pl.when(even_row)
+        def _():
+            xret_out[g] = above.astype(BF)
+            part[g] = below
+
+        @pl.when(jnp.logical_not(even_row))
+        def _():
+            xret_out[g] = below.astype(BF)
+            part[g] = above
+
+        @pl.when(has_last)
+        def _():
+            x_return(g).start()
+
+    def send_partner(g):
+        @pl.when(has_next)
+        def _():
+            x_return(g).wait_recv()
+
+        mine, other = part[g], xret_in[g].astype(F32)
+        first, second = jnp.where(even_row, mine, other), jnp.where(even_row, other, mine)
+        cut, tail = OWN - STRIP, 2 * STRIP - OWN
+        zret_out[g] = jnp.concatenate(
+            [first[:cut], first[cut:] + second[:tail], second[tail:]], axis=0
+        ).astype(BF)
+        z_return(g).start()
 
     def hand_rows(g):
-        for way, mine in ((0, jnp.logical_not(even_row)), (1, even_row)):
-            @pl.when(mine & hands_on(g))
-            def _():
-                for copy in v_forward_first(g, way):
-                    copy.wait_recv()
-                for copy in v_forward_second(g, way):
-                    copy.start()
-
-    def hand_rows_back(g):
-        for way, mine in ((0, jnp.logical_not(even_row)), (1, even_row)):
-            @pl.when(mine & hands_on(g))
-            def _():
-                v_return_first(g, way).wait_recv()
-                v_return_second(g, way).start()
+        for copy in z_forward(g):
+            copy.wait_recv()
+
+        @pl.when(has_next)
+        def _():
+            x_forward(g).start()
 
     def hand_sides(g):
         for way in range(2):
@@ -518,22 +520,18 @@
         stage(-1, hand_rows)
         stage(1, hand_sides)
         stage(0, send_sides)
-        stage(3, attend)
-        stage(4, hand_sides_back)
-        stage(5, send_rows)
-        stage(6, hand_rows_back)
+        stage(2, attend)
+        stage(3, hand_sides_back)
+        stage(4, send_rows)
+        stage(5, send_partner)
         return carry
 
     hand_rows(0)
-    lax.fori_loop(0, groups + 6, step, 0)
+    lax.fori_loop(0, groups + 5, step, 0)
 
     def finish(g, carry):
-        for way in range(2):
-            @pl.when(v_from[way])
-            def _():
-                v_return(g, way).wait_recv()
-        own[g, pl.ds(OWN - STRIP, STRIP), :] += vret_in[g, 0].astype(F32)
-        own[g, pl.ds(0, STRIP), :] += vret_in[g, 1].astype(F32)
+        z_return(g).wait_recv()
+        own[g] += zret_in[g].astype(F32)
         dk_buf[g] = own[g, :, pl.ds(0, LANES)].astype(BF)
         dv_buf[g] = own[g, :, pl.ds(LANES, LANES)].astype(BF)
         store(g, 2).start()
@@ -545,23 +543,23 @@
     def drain(g, carry):
         for n in range(4):
             store(g, n).wait()
+        for copy in z_forward(g):
+            copy.wait_send()
+        z_return(g).wait_send()
+
+        @pl.when(has_next)
+        def _():
+            x_forward(g).wait_send()
+
+        @pl.when(has_last)
+        def _():
+            x_return(g).wait_send()
+
         for way in range(2):
-            @pl.when(v_to[way])
-            def _():
-                for copy in v_forward(g, way):
-                    copy.wait_send()
-                v_return(g, way).wait_send()
-
             @pl.when(h_to[way])
             def _():
                 h_forward(g, way).wait_send()
                 h_return(g, way).wait_send()
-
-        @pl.when(hands_on(g))
-        def _():
-            for copy in v_forward_second(g, 0):
-                copy.wait_send()
-            v_return_second(g, 0).wait_send()
 
         @pl.when(hands_sides(g, 0) | hands_sides(g, 1))
         def _():
@@ -606,7 +604,7 @@
         in_specs=[any_spec] * 4 + [pl.BlockSpec(memory_space=pltpu.VMEM)],
         out_specs=[any_spec] * 4,
         scratch_shapes=[
-            pltpu.VMEM((groups, KEYS, 2 * LANES), BF),
+            pltpu.VMEM((groups, ROWS, 2 * LANES), BF),
             pltpu.VMEM((groups, OWN, LANES), BF),
             pltpu.VMEM((groups, OWN, LANES), BF),
             pltpu.VMEM((KEYS, LANES), BF),
@@ -619,25 +617,24 @@
             pltpu.VMEM((groups, 2 * SLOTS, 2 * LANES), BF),
             pltpu.VMEM((3, CENTER, 2 * LANES), F32),
             pltpu.VMEM((groups, OWN, 2 * LANES), F32),
+            pltpu.VMEM((groups, STRIP, 2 * LANES), F32),
             pltpu.VMEM((groups, 2 * SLOTS, 2 * LANES), BF),
             pltpu.VMEM((groups, 2 * SLOTS, 2 * LANES), BF),
-            pltpu.VMEM((groups, 2, STRIP, 2 * LANES), BF),
-            pltpu.VMEM((groups, 2, STRIP, 2 * LANES), BF),
+            pltpu.VMEM((groups, STRIP, 2 * LANES), BF),
+            pltpu.VMEM((groups, STRIP, 2 * LANES), BF),
+            pltpu.VMEM((groups, OWN, 2 * LANES), BF),
+            pltpu.VMEM((groups, OWN, 2 * LANES), BF),
             pltpu.VMEM((groups, OWN, LANES), BF),
             pltpu.VMEM((groups, OWN, LANES), BF),
             pltpu.VMEM((groups, OWN, LANES), BF),
             pltpu.VMEM((groups, OWN, LANES), BF),
-            pltpu.VMEM((groups, STRIP, 2 * LANES), BF),
-            pltpu.VMEM((groups, STRIP, 2 * LANES), BF),
             pltpu.VMEM((groups, SLOTS, 2 * LANES), BF),
             pltpu.VMEM((groups, SLOTS, 2 * LANES), BF),
             dma((groups, 4)), dma((groups, 4)),
-            dma((groups, 2, 2)), dma((groups, 2, 2)),
-            dma((groups, 2)), dma((groups, 2)),
-            dma((groups, 2)), dma((groups, 2)),
-            dma((groups, 2)), dma((groups, 2)),
+            dma((groups, 2)), dma((groups, 2)), dma((groups,)), dma((groups,)),
+            dma((groups, 2)), dma((groups, 2)), dma((groups, 2)), dma((groups, 2)),
+            dma((groups,)), dma((groups,)), dma((groups,)), dma((groups,)),
             dma((2,)), dma((2,)), dma((2,)), dma((2,)),
-            dma((groups, 2)), dma((groups, 2)), dma((groups,)), dma((groups,)),
             dma((groups,)), dma((groups,)), dma((groups,)), dma((groups,)),
         ],
         compiler_params=pltpu.CompilerParams(

time: 83.7 us -> 70.5 us (0.84); the launches traced: 82.1 us -> 70.3 us
  Pallas kernels: 81.5 us -> 69.7 us
    pallas_call x1, Pallas kernels: 79 us -> 67.3 us  [per_device(): pl.pallas_call(functools.partial(kernel, groups, lax.axis_size('gx'), lax...]
where the time goes in v2:
time: 70.5 us; the launch traced here: 70.3 us
  Pallas kernels  69.7 us (99%)
    pallas_call x1, Pallas kernels, per_device(): pl.pallas_call(functools.partial(kernel, groups, lax.axis_size('gx'), lax...  67.3 us
    pallas_call x1, Pallas kernels, per_device(): pl.pallas_call(write_out, out_shape=[jax.ShapeDtypeStruct(flat, BF)] * 4,...  2.42 us

profile of v2, /device:TPU:6, one launch (start us, length us, event | category | flops | bytes accessed | tf_op | source)
XLA Modules:
  0.0 70.3 jit_solution(1390464497987741675)
XLA Ops:
  0.6 67.3 %shard_map.84 = (bf16[256,1024]{1,0:T(8,128)(2,1)}, bf16[256,1024]{1,0:T(8,128)(2,1)}, bf16[256,1024]{1,0:T(8,128)(2,1)}, bf16[256,1024]{1,0:T(8,128)(2,1)}) custom-call(bf16[256,1024]{1,0:T(8,128)(2,1)} %bitcast.8, bf16[256,1024]{1,0:T(8,128)(2,1)} %bitcast.9, bf16[256,1024]{1,0:T(8,128)(2,1)} %bitcast.10, bf16[256,1024]{1,0:T(8,128)(2,1)} %bitcast.11, ...), custom_call_target="tpu_custom_call" | custom-call | tf_op jit(solution)/shard_map/pallas_call | solution.py:601
  67.9 2.4 %shard_map.85 = (bf16[256,1024]{1,0:T(8,128)(2,1)}, bf16[256,1024]{1,0:T(8,128)(2,1)}, bf16[256,1024]{1,0:T(8,128)(2,1)}, bf16[256,1024]{1,0:T(8,128)(2,1)}) custom-call(bf16[256,1024]{1,0:T(8,128)(2,1)} %get-tuple-element.12.refs_0_, bf16[256,1024]{1,0:T(8,128)(2,1)} %get-tuple-element.13.refs_1_, bf16[256,1024]{1,0:T(8,128)(2,1)} %get-tuple-element.14.refs_2_, ...), custom_call_target="tpu_custom_call" | custom-call | tf_op jit(solution)/shard_map/pallas_call | solution.py:647

commit v3 on v2

--- a/solution.py
+++ b/solution.py
@@ -22,6 +22,8 @@
 TOP = OWN - STRIP
 SIDES = 3 * OWN
 ROWS = SIDES + 2 * SLOTS
+HALF = OWN // 2
+REACH = HALF + 2 * STRIP
 FAR = -1e30
 LEAD = 3
 RATE = 1
@@ -238,13 +240,6 @@
         for copy in z_forward(g):
             copy.start()
 
-    def start_loads(g, carry):
-        for copy in loads(g):
-            copy.start()
-        return carry
-
-    lax.fori_loop(0, groups, start_loads, 0)
-
     dead32[...] = jnp.ones_like(dead32)
     dead32[pl.ds(0, TH), pl.ds(0, TW)] = jnp.where(tissue_ref[...] > 0, 0.0, 1.0)
     dead[...] = jnp.zeros_like(dead)
@@ -256,6 +251,18 @@
         def _():
             dead[tile, pl.ds(first, count), :] = jnp.ones((count, LANES), BF)
 
+    barrier = pltpu.get_barrier_semaphore()
+    for here, where in sides:
+        @pl.when(here)
+        def _():
+            pl.semaphore_signal(barrier, inc=1, device_id=where, device_id_type=MESH)
+    def start_loads(g, carry):
+        for copy in loads(g):
+            copy.start()
+        return carry
+
+    lax.fori_loop(0, groups, start_loads, 0)
+
     for here, first, count in (
         (has_up, TOP, STRIP), (has_down, 2 * OWN, STRIP),
         (has_left, SIDES, SLOTS), (has_right, SIDES + SLOTS, SLOTS),
@@ -285,11 +292,6 @@
 
             lax.fori_loop(0, groups, clear, 0)
 
-    barrier = pltpu.get_barrier_semaphore()
-    for here, where in sides:
-        @pl.when(here)
-        def _():
-            pl.semaphore_signal(barrier, inc=1, device_id=where, device_id_type=MESH)
     peers = sum(here.astype(jnp.int32) for here, _ in sides)
     pl.semaphore_wait(barrier, peers)
 
@@ -367,57 +369,84 @@
             @pl.when(h_from[way])
             def _():
                 h_forward(g, way).wait_recv()
-        key_all, value_all = (
-            jnp.concatenate(
-                [kv[g, pl.ds(TOP, CENTER), pl.ds(n, LANES)], kv[g, pl.ds(SIDES, 2 * SLOTS), pl.ds(n, LANES)]],
-                axis=0,
-            )
-            for n in (0, LANES)
-        )
-        key_t, value_t = key_all.T, value_all.T
+        contract = (((1,), (1,)), ((), ()))
         query = q_buf[g] * (HD ** -0.5)
         grad = g_buf[g]
-        grad_t = grad.T.astype(F32)
-        with_feat = jnp.concatenate([key_all, feat[...]], axis=1)
         head_of = iota((OWN, LANES), 1) // HD
         nothing = jnp.zeros((OWN, LANES), BF)
-        live_row = live_q[pl.ds(0, 1), :]
-        contract = (((1,), (1,)), ((), ()))
-        parts = [slice(head * HD, (head + 1) * HD) for head in range(2)]
         queries_h = [jnp.where(head_of == head, query, nothing) for head in range(2)]
         grads_h = [jnp.where(head_of == head, grad, nothing) for head in range(2)]
-
-        def scores_of(head):
+        grad_t = grad.T.astype(F32)
+        side_keys, side_values = (kv[g, pl.ds(SIDES, 2 * SLOTS), pl.ds(n, LANES)] for n in (0, LANES))
+        mid_keys, mid_values = (kv[g, pl.ds(TOP, CENTER), pl.ds(n, LANES)] for n in (0, LANES))
+        side_keys_t, side_values_t = side_keys.T, side_values.T
+        mid_keys_t, mid_values_t = mid_keys.T, mid_values.T
+
+        def tokens_of(half):
+            return slice(half * HALF, (half + 1) * HALF)
+
+        def reach_of(half):
+            return slice(half * HALF, half * HALF + REACH)
+
+        def both(pair, half):
+            return jnp.concatenate([x[tokens_of(half)] for x in pair], axis=0)
+
+        def keys_of(half, mid, side):
+            return jnp.concatenate([mid[reach_of(half)], side], axis=0)
+
+        def keys_t_of(half, mid, side):
+            return jnp.concatenate([mid[:, reach_of(half)], side], axis=1)
+
+        def scores_of(half):
+            feats = keys_of(half, feat[pl.ds(0, CENTER), :], feat[pl.ds(CENTER, 2 * SLOTS), :])
+            own_feats = qfeat[pl.ds(half * HALF, HALF), :]
             return lax.dot_general(
-                with_feat, jnp.concatenate([queries_h[head], qfeat[...]], axis=1), contract,
-                preferred_element_type=F32,
-            )
-
-        def attention_of(scores):
+                jnp.concatenate([keys_of(half, mid_keys, side_keys), feats], axis=1),
+                jnp.concatenate(
+                    [both(queries_h, half), jnp.concatenate([own_feats, own_feats], axis=0)], axis=1
+                ),
+                contract, preferred_element_type=F32,
+            )
+
+        def attention_of(half, scores):
+            live = live_q[pl.ds(0, 1), pl.ds(half * HALF, HALF)]
             top = jnp.max(scores, axis=0, keepdims=True)
             raised = jnp.exp(scores - top)
             total = jnp.sum(raised, axis=0, keepdims=True)
-            return raised * (live_row / total)
-
-        def attended_of(head, weight):
-            out = jnp.dot(value_t[parts[head]], weight, preferred_element_type=F32)
-            return out.astype(BF).astype(F32)
-
-        def delta_of(head, out):
-            return jnp.sum(out * grad_t[parts[head]], axis=0, keepdims=True)
-
-        def grad_prob_of(head):
-            return lax.dot_general(value_all, grads_h[head], contract, preferred_element_type=F32)
-
-        def query_grad_of(head, grad_score):
-            return jnp.dot(key_t[parts[head]], grad_score, preferred_element_type=F32)
+            return raised * (jnp.concatenate([live, live], axis=1) / total)
+
+        def per_head(out):
+            return jnp.concatenate([out[:HD, :HALF], out[HD:, HALF:]], axis=0)
+
+        def attended_of(half, weight):
+            out = jnp.dot(
+                keys_t_of(half, mid_values_t, side_values_t), weight, preferred_element_type=F32
+            )
+            return per_head(out).astype(BF).astype(F32)
+
+        def delta_of(half, out):
+            terms = out * grad_t[:, tokens_of(half)]
+            return jnp.concatenate(
+                [jnp.sum(terms[:HD], axis=0, keepdims=True), jnp.sum(terms[HD:], axis=0, keepdims=True)], axis=1
+            )
+
+        def grad_prob_of(half):
+            return lax.dot_general(
+                keys_of(half, mid_values, side_values), both(grads_h, half), contract,
+                preferred_element_type=F32,
+            )
+
+        def query_grad_of(half, grad_score):
+            return per_head(
+                jnp.dot(keys_t_of(half, mid_keys_t, side_keys_t), grad_score, preferred_element_type=F32)
+            )
 
         scores_0, scores_1 = scores_of(0), scores_of(1)
-        attention_0 = attention_of(scores_0)
+        attention_0 = attention_of(0, scores_0)
         weight_0 = attention_0.astype(BF)
         prob_0 = grad_prob_of(0)
         out_0 = attended_of(0, weight_0)
-        attention_1 = attention_of(scores_1)
+        attention_1 = attention_of(1, scores_1)
         weight_1 = attention_1.astype(BF)
         prob_1 = grad_prob_of(1)
         delta_0 = delta_of(0, out_0)
@@ -427,21 +456,24 @@
         query_grad_0 = query_grad_of(0, score_0)
         score_1 = (attention_1 * (prob_1 - delta_1)).astype(BF)
         query_grad_1 = query_grad_of(1, score_1)
-        key_grad = jnp.dot(
-            jnp.concatenate([score_0, score_1], axis=1), jnp.concatenate(queries_h, axis=0),
-            preferred_element_type=F32,
-        )
-        value_grad = jnp.dot(
-            jnp.concatenate([weight_0, weight_1], axis=1), jnp.concatenate(grads_h, axis=0),
-            preferred_element_type=F32,
-        )
-        o_buf[g] = jnp.concatenate([out_0, out_1], axis=0).T.astype(BF)
-        dq_buf[g] = (jnp.concatenate([query_grad_0, query_grad_1], axis=0) * (HD ** -0.5)).T.astype(BF)
+
+        def key_sums(factors, rows_h):
+            first, second = (
+                jnp.dot(factor, both(rows_h, half), preferred_element_type=F32)
+                for half, factor in enumerate(factors)
+            )
+            middle = first[HALF:REACH] + second[: REACH - HALF]
+            mid = jnp.concatenate([first[:HALF], middle, second[REACH - HALF : REACH]], axis=0)
+            return mid, first[REACH:] + second[REACH:]
+
+        key_mid, key_side = key_sums((score_0, score_1), queries_h)
+        value_mid, value_side = key_sums((weight_0, weight_1), grads_h)
+        o_buf[g] = jnp.concatenate([out_0, out_1], axis=1).T.astype(BF)
+        dq_buf[g] = (jnp.concatenate([query_grad_0, query_grad_1], axis=1) * (HD ** -0.5)).T.astype(BF)
         store(g, 0).start()
         store(g, 1).start()
-        sums = jnp.concatenate([key_grad, value_grad], axis=1)
-        centre[lax.rem(g, 3)] = sums[:CENTER]
-        hret_out[g] = sums[CENTER:].astype(BF)
+        centre[lax.rem(g, 3)] = jnp.concatenate([key_mid, value_mid], axis=1)
+        hret_out[g] = jnp.concatenate([key_side, value_side], axis=1).astype(BF)
         for way in range(2):
             send(
                 h_to[way], at_seam[way] & side_picked(g),
@@ -529,23 +561,11 @@
     hand_rows(0)
     lax.fori_loop(0, groups + 5, step, 0)
 
-    def finish(g, carry):
-        z_return(g).wait_recv()
-        own[g] += zret_in[g].astype(F32)
-        dk_buf[g] = own[g, :, pl.ds(0, LANES)].astype(BF)
-        dv_buf[g] = own[g, :, pl.ds(LANES, LANES)].astype(BF)
-        store(g, 2).start()
-        store(g, 3).start()
-        return carry
-
-    lax.fori_loop(0, groups, finish, 0)
-
     def drain(g, carry):
-        for n in range(4):
-            store(g, n).wait()
+        store(g, 0).wait()
+        store(g, 1).wait()
         for copy in z_forward(g):
             copy.wait_send()
-        z_return(g).wait_send()
 
         @pl.when(has_next)
         def _():
@@ -577,6 +597,25 @@
         @pl.when(h_to[way])
         def _():
             live_h(way).wait_send()
+
+    def finish(g, carry):
+        z_return(g).wait_recv()
+        total = own[g] + zret_in[g].astype(F32)
+        dk_buf[g] = total[:, :LANES].astype(BF)
+        dv_buf[g] = total[:, LANES:].astype(BF)
+        store(g, 2).start()
+        store(g, 3).start()
+        return carry
+
+    lax.fori_loop(0, groups, finish, 0)
+
+    def drain_last(g, carry):
+        z_return(g).wait_send()
+        store(g, 2).wait()
+        store(g, 3).wait()
+        return carry
+
+    lax.fori_loop(0, groups, drain_last, 0)
 
 
 def write_out(*refs):

time: 70.5 us -> 69.9 us (level)
  no operation moved by 1% of the time
where the time goes in v3:
time: 69.9 us; the launch traced here: 69.7 us
  Pallas kernels  69.1 us (99%)
    pallas_call x1, Pallas kernels, per_device(): pl.pallas_call(functools.partial(kernel, groups, lax.axis_size('gx'), lax...  66.6 us
    pallas_call x1, Pallas kernels, per_device(): pl.pallas_call(write_out, out_shape=[jax.ShapeDtypeStruct(flat, BF)] * 4,...  2.42 us

profile of v3, /device:TPU:6, one launch (start us, length us, event | category | flops | bytes accessed | tf_op | source)
XLA Modules:
  0.0 69.7 jit_solution(12577365977305619888)
XLA Ops:
  0.6 66.6 %shard_map.84 = (bf16[256,1024]{1,0:T(8,128)(2,1)}, bf16[256,1024]{1,0:T(8,128)(2,1)}, bf16[256,1024]{1,0:T(8,128)(2,1)}, bf16[256,1024]{1,0:T(8,128)(2,1)}) custom-call(bf16[256,1024]{1,0:T(8,128)(2,1)} %bitcast.8, bf16[256,1024]{1,0:T(8,128)(2,1)} %bitcast.9, bf16[256,1024]{1,0:T(8,128)(2,1)} %bitcast.10, bf16[256,1024]{1,0:T(8,128)(2,1)} %bitcast.11, ...), custom_call_target="tpu_custom_call" | custom-call | tf_op jit(solution)/shard_map/pallas_call | solution.py:640
  67.3 2.4 %shard_map.85 = (bf16[256,1024]{1,0:T(8,128)(2,1)}, bf16[256,1024]{1,0:T(8,128)(2,1)}, bf16[256,1024]{1,0:T(8,128)(2,1)}, bf16[256,1024]{1,0:T(8,128)(2,1)}) custom-call(bf16[256,1024]{1,0:T(8,128)(2,1)} %get-tuple-element.12.refs_0_, bf16[256,1024]{1,0:T(8,128)(2,1)} %get-tuple-element.13.refs_1_, bf16[256,1024]{1,0:T(8,128)(2,1)} %get-tuple-element.14.refs_2_, ...), custom_call_target="tpu_custom_call" | custom-call | tf_op jit(solution)/shard_map/pallas_call | solution.py:686

commit v4 on v3

--- a/solution.py
+++ b/solution.py
@@ -74,11 +74,11 @@
     kv, q_buf, g_buf, feat, qfeat, sel, sel_t, dead, dead32, live_q,
     hsend, centre, own, part, hret_out, hret_in, xret_out, xret_in, zret_out, zret_in,
     o_buf, dq_buf, dk_buf, dv_buf,
-    side_relay, side_relay_back,
+    side_relay_back,
     in_sem, out_sem, zf_send, zf_recv, xf_send, xf_recv, hf_send, hf_recv, hr_send, hr_recv,
     xr_send, xr_recv, zr_send, zr_recv,
     lv_send, lv_recv, lh_send, lh_recv,
-    sf_send, sf_recv, sb_send, sb_recv,
+    sb_send, sb_recv,
 ):
     gx, gy = lax.axis_index("gx"), lax.axis_index("gy")
     has_up, has_down = gy > 0, gy < ny - 1
@@ -170,18 +170,6 @@
     def z_return(g):
         return remote(zret_out.at[g], zret_in.at[g], zr_send.at[g], zr_recv.at[g], partner)
 
-    def h_forward_first(g, way):
-        return remote(
-            hsend.at[g, pl.ds(way * SLOTS, SLOTS)], side_relay.at[g],
-            hf_send.at[g, way], sf_recv.at[g], relay_of(g, way),
-        )
-
-    def h_forward_second(g, way):
-        to_rows = pl.ds(SIDES + (1 - way) * SLOTS, SLOTS)
-        return remote(
-            side_relay.at[g], kv.at[g, to_rows], sf_send.at[g], hf_recv.at[g, way], seam_to[way],
-        )
-
     def h_return_first(g, way):
         return remote(
             hret_out.at[g, pl.ds(way * SLOTS, SLOTS)], side_relay_back.at[g],
@@ -359,10 +347,9 @@
         picked = jnp.dot(sel[...], kv[g, pl.ds(TOP, CENTER), :], preferred_element_type=F32)
         hsend[g] = picked.astype(BF)
         for way in range(2):
-            send(
-                h_to[way], at_seam[way] & side_picked(g),
-                lambda: [h_forward(g, way)], lambda: [h_forward_first(g, way)],
-            )
+            @pl.when(h_to[way])
+            def _():
+                h_forward(g, way).start()
 
     def attend(g):
         for way in range(2):
@@ -524,13 +511,6 @@
         def _():
             x_forward(g).start()
 
-    def hand_sides(g):
-        for way in range(2):
-            @pl.when(hands_sides(g, way))
-            def _():
-                h_forward_first(g, way).wait_recv()
-                h_forward_second(g, way).start()
-
     def hand_sides_back(g):
         for way in range(2):
             @pl.when(hands_sides(g, way))
@@ -550,7 +530,6 @@
                 start_rows(LEAD + RATE * i + n)
 
         stage(-1, hand_rows)
-        stage(1, hand_sides)
         stage(0, send_sides)
         stage(2, attend)
         stage(3, hand_sides_back)
@@ -583,7 +562,6 @@
 
         @pl.when(hands_sides(g, 0) | hands_sides(g, 1))
         def _():
-            h_forward_second(g, 0).wait_send()
             h_return_second(g, 0).wait_send()
 
         return carry
@@ -668,13 +646,12 @@
             pltpu.VMEM((groups, OWN, LANES), BF),
             pltpu.VMEM((groups, OWN, LANES), BF),
             pltpu.VMEM((groups, SLOTS, 2 * LANES), BF),
-            pltpu.VMEM((groups, SLOTS, 2 * LANES), BF),
             dma((groups, 4)), dma((groups, 4)),
             dma((groups, 2)), dma((groups, 2)), dma((groups,)), dma((groups,)),
             dma((groups, 2)), dma((groups, 2)), dma((groups, 2)), dma((groups, 2)),
             dma((groups,)), dma((groups,)), dma((groups,)), dma((groups,)),
             dma((2,)), dma((2,)), dma((2,)), dma((2,)),
-            dma((groups,)), dma((groups,)), dma((groups,)), dma((groups,)),
+            dma((groups,)), dma((groups,)),
         ],
         compiler_params=pltpu.CompilerParams(
             collective_id=0, has_side_effects=True, vmem_limit_bytes=56 * 1024 * 1024

time: 69.9 us -> 68.5 us (0.980)
  Pallas kernels: 69.1 us -> 67.2 us
    pallas_call x1, Pallas kernels: 66.6 us -> 64.8 us  [per_device(): pl.pallas_call(functools.partial(kernel, groups, lax.axis_size('gx'), lax...]
where the time goes in v4:
time: 68.5 us; the launch traced here: 67.9 us
  Pallas kernels  67.2 us (98%)
    pallas_call x1, Pallas kernels, per_device(): pl.pallas_call(functools.partial(kernel, groups, lax.axis_size('gx'), lax...  64.8 us
    pallas_call x1, Pallas kernels, per_device(): pl.pallas_call(write_out, out_shape=[jax.ShapeDtypeStruct(flat, BF)] * 4,...  2.42 us

profile of v4, /device:TPU:6, one launch (start us, length us, event | category | flops | bytes accessed | tf_op | source)
XLA Modules:
  0.0 67.9 jit_solution(9244717141386143923)
XLA Ops:
  0.6 64.8 %shard_map.84 = (bf16[256,1024]{1,0:T(8,128)(2,1)}, bf16[256,1024]{1,0:T(8,128)(2,1)}, bf16[256,1024]{1,0:T(8,128)(2,1)}, bf16[256,1024]{1,0:T(8,128)(2,1)}) custom-call(bf16[256,1024]{1,0:T(8,128)(2,1)} %bitcast.8, bf16[256,1024]{1,0:T(8,128)(2,1)} %bitcast.9, bf16[256,1024]{1,0:T(8,128)(2,1)} %bitcast.10, bf16[256,1024]{1,0:T(8,128)(2,1)} %bitcast.11, ...), custom_call_target="tpu_custom_call" | custom-call | tf_op jit(solution)/shard_map/pallas_call | solution.py:618
  65.4 2.4 %shard_map.85 = (bf16[256,1024]{1,0:T(8,128)(2,1)}, bf16[256,1024]{1,0:T(8,128)(2,1)}, bf16[256,1024]{1,0:T(8,128)(2,1)}, bf16[256,1024]{1,0:T(8,128)(2,1)}) custom-call(bf16[256,1024]{1,0:T(8,128)(2,1)} %get-tuple-element.12.refs_0_, bf16[256,1024]{1,0:T(8,128)(2,1)} %get-tuple-element.13.refs_1_, bf16[256,1024]{1,0:T(8,128)(2,1)} %get-tuple-element.14.refs_2_, ...), custom_call_target="tpu_custom_call" | custom-call | tf_op jit(solution)/shard_map/pallas_call | solution.py:663

commit v5 on v4

--- a/solution.py
+++ b/solution.py
@@ -598,8 +598,9 @@
 
 def write_out(*refs):
     ins, outs, bufs, sem = refs[:4], refs[4:8], refs[8:12], refs[12]
-    reads = [pltpu.make_async_copy(a, b, sem.at[0, n]) for n, (a, b) in enumerate(zip(ins, bufs))]
-    writes = [pltpu.make_async_copy(a, b, sem.at[1, n]) for n, (a, b) in enumerate(zip(bufs, outs))]
+    cuts = [(n, c, pl.ds(c * (OWN // 4), OWN // 4)) for c in range(4) for n in range(4)]
+    reads = [pltpu.make_async_copy(ins[n].at[at], bufs[n].at[at], sem.at[0, n, c]) for n, c, at in cuts]
+    writes = [pltpu.make_async_copy(bufs[n].at[at], outs[n].at[at], sem.at[1, n, c]) for n, c, at in cuts]
     for copy in reads:
         copy.start()
     for read, write in zip(reads, writes):
@@ -665,7 +666,7 @@
         out_shape=[jax.ShapeDtypeStruct(flat, BF)] * 4,
         in_specs=[any_spec] * 4,
         out_specs=[any_spec] * 4,
-        scratch_shapes=[pltpu.VMEM(flat, BF)] * 4 + [dma((2, 4))],
+        scratch_shapes=[pltpu.VMEM(flat, BF)] * 4 + [dma((2, 4, 4))],
     )(*outs)
     return tuple(out.reshape(queries.shape) for out in outs)
 

time: 68.5 us -> 68.7 us (level)
  no operation moved by 1% of the time
where the time goes in v5:
time: 68.7 us; the launch traced here: 68 us
  Pallas kernels  67.4 us (98%)
    pallas_call x1, Pallas kernels, per_device(): pl.pallas_call(functools.partial(kernel, groups, lax.axis_size('gx'), lax...  64.8 us
    pallas_call x1, Pallas kernels, per_device(): pl.pallas_call(write_out, out_shape=[jax.ShapeDtypeStruct(flat, BF)] * 4,...  2.57 us

profile of v5, /device:TPU:6, one launch (start us, length us, event | category | flops | bytes accessed | tf_op | source)
XLA Modules:
  0.0 68.0 jit_solution(5191484382025619134)
XLA Ops:
  0.6 64.8 %shard_map.84 = (bf16[256,1024]{1,0:T(8,128)(2,1)}, bf16[256,1024]{1,0:T(8,128)(2,1)}, bf16[256,1024]{1,0:T(8,128)(2,1)}, bf16[256,1024]{1,0:T(8,128)(2,1)}) custom-call(bf16[256,1024]{1,0:T(8,128)(2,1)} %bitcast.8, bf16[256,1024]{1,0:T(8,128)(2,1)} %bitcast.9, bf16[256,1024]{1,0:T(8,128)(2,1)} %bitcast.10, bf16[256,1024]{1,0:T(8,128)(2,1)} %bitcast.11, ...), custom_call_target="tpu_custom_call" | custom-call | tf_op jit(solution)/shard_map/pallas_call | solution.py:619
  65.4 2.6 %shard_map.85 = (bf16[256,1024]{1,0:T(8,128)(2,1)}, bf16[256,1024]{1,0:T(8,128)(2,1)}, bf16[256,1024]{1,0:T(8,128)(2,1)}, bf16[256,1024]{1,0:T(8,128)(2,1)}) custom-call(bf16[256,1024]{1,0:T(8,128)(2,1)} %get-tuple-element.12.refs_0_, bf16[256,1024]{1,0:T(8,128)(2,1)} %get-tuple-element.13.refs_1_, bf16[256,1024]{1,0:T(8,128)(2,1)} %get-tuple-element.14.refs_2_, ...), custom_call_target="tpu_custom_call" | custom-call | tf_op jit(solution)/shard_map/pallas_call | solution.py:664
